TPU v7x, 32 devices: a whole 2x2x4 slice. The times are simulated.
32 devices in a mesh: clus: 8 (over z, y), rhs: 4 (over x, core).
Axes of the slice: x: 2, y: 2, z: 4, core: 2. Of those that a mesh axis runs over, the one named last changes fastest.
Arguments:
- rhs_in: bfloat16 [2, 32, 4096], P(None, 'rhs', 'clus'), may hold values from -6 to 6
- row_basis: bfloat16 [16, 2, 96, 256], P('clus'), may hold values from -0.25 to 0.25
- col_basis: bfloat16 [16, 2, 96, 256], P('clus'), may hold values from -0.09375 to 0.09375
- coupling: bfloat16 [16, 24, 96, 192], P('clus', 'rhs'), may hold values from -0.4375 to 0.4375
- far_col: int32 [16, 24], P('clus', 'rhs'), may hold values from 0 to 15, as said below
- cluster_rank: int32 [16], P('clus'), may hold values from 32 to 96
- near_block: bfloat16 [16, 16, 2, 256, 256], P('clus', 'rhs'), may hold values from -0.0625 to 0.0625
- near_col: int32 [16, 16], P('clus', 'rhs'), may hold values from 0 to 15, as said below
Outputs:
- adjoint_out: bfloat16 [2, 32, 4096], P(None, 'rhs', 'clus')
Inputs may be any that keep to these rules, and one draw needn't show every extreme that they name: `near_col`: each entry lies within 2 clusters of its own row cluster; slot 0 is the row cluster itself and slot 1 lies exactly 2 clusters away from it. `far_col`: of the far blocks held by one device (rows of 2 row clusters, 24 / 4 blocks each), at most 2 have column clusters in the same aligned group of 2 clusters c * 2 to (c + 1) * 2 - 1, and some group receives exactly 2.
All inputs are finite; a program needn't handle non-finite values.
Results may differ from a plain program's by a relative error of at most 0.0044.
Values may be sent and summed in bfloat16 or wider, within the bound.
A program may use at most 64 MiB of HBM per device.

v0:
```python
import jax
import jax.numpy as jnp
from jax import lax
from jax.sharding import PartitionSpec as P


def extended_2(array, sides, width):
    for axis, dim in sides:
        size, length = (lax.axis_size(axis), array.shape[dim])
        up = [(i, (i + 1) % size) for i in range(size - 1)]
        down = [(j, i) for i, j in up]
        last = lax.slice_in_dim(array, length - width, length, axis=dim)
        first = lax.slice_in_dim(array, 0, width, axis=dim)
        before = lax.ppermute(last, axis, up)
        after = lax.ppermute(first, axis, down)
        array = jnp.concatenate([before, array, after], axis=dim)
    return array


def body(rhs_in, row_basis, col_basis, coupling, far_col, cluster_rank, near_block, near_col):
    rhs_all = lax.all_gather(rhs_in, "rhs", axis=1, tiled=True)
    local_count, _, rank_width, leaf_size = row_basis.shape
    full_width = rhs_all.shape[1]
    rhs_groups = lax.axis_size("rhs")
    clus_groups = lax.axis_size("clus")
    narrow_width = full_width // rhs_groups
    total_clusters = local_count * clus_groups
    first_cluster = lax.axis_index("clus") * local_count
    field_rows = rhs_all.reshape(2, full_width, local_count, leaf_size)
    rank_keep = (jnp.arange(rank_width)[None, :] < cluster_rank[:, None]).astype(jnp.float32)
    projected = jnp.einsum(
        "prcm,cqkm->cpqrk", field_rows, row_basis, preferred_element_type=jnp.float32
    )
    coeff_re = projected[:, 0, 0] - projected[:, 1, 1]
    coeff_im = projected[:, 0, 1] + projected[:, 1, 0]
    basis_coeff = (jnp.stack([coeff_re, coeff_im], axis=1) * rank_keep[:, None, None, :]).astype(
        jnp.bfloat16
    )
    coupled = jnp.einsum(
        "cprk,cfkl->cfprl", basis_coeff, coupling, preferred_element_type=jnp.float32
    )
    term_re = coupled[:, :, 0, :, :rank_width] - coupled[:, :, 1, :, rank_width:]
    term_im = coupled[:, :, 0, :, rank_width:] + coupled[:, :, 1, :, :rank_width]
    far_terms = jnp.stack([term_re, term_im], axis=2).reshape(-1, 2 * full_width * rank_width)
    block_cols = far_col.reshape(-1)
    far_select = (jnp.arange(total_clusters)[:, None] == block_cols[None, :]).astype(jnp.float32)
    far_partial = jnp.dot(far_select, far_terms, precision=lax.Precision.HIGHEST)
    arranged = far_partial.reshape(
        clus_groups, local_count, 2, rhs_groups, narrow_width, rank_width
    )
    arranged = arranged.transpose(0, 3, 1, 2, 4, 5).reshape(
        clus_groups * rhs_groups, local_count * 2 * narrow_width * rank_width
    )
    far_sum = lax.psum_scatter(arranged, ("clus", "rhs"), scatter_dimension=0, tiled=True)
    far_sum = far_sum.reshape(local_count, 2, narrow_width, rank_width)
    far_coeff = (far_sum * rank_keep[:, None, None, :]).astype(jnp.bfloat16)
    far_proj = jnp.einsum(
        "cprk,cqkm->cpqrm", far_coeff, col_basis, preferred_element_type=jnp.float32
    )
    far_field = jnp.stack(
        [far_proj[:, 0, 0] - far_proj[:, 1, 1], far_proj[:, 0, 1] + far_proj[:, 1, 0]], axis=1
    )
    near_proj = jnp.einsum(
        "prcm,cnqml->cnpqrl", field_rows, near_block, preferred_element_type=jnp.float32
    )
    near_terms = jnp.stack(
        [
            near_proj[:, :, 0, 0] - near_proj[:, :, 1, 1],
            near_proj[:, :, 0, 1] + near_proj[:, :, 1, 0],
        ],
        axis=2,
    )
    near_terms = near_terms.reshape(-1, 2 * full_width * leaf_size)
    band_place = near_col.reshape(-1) - first_cluster + local_count
    band_select = (jnp.arange(3 * local_count)[:, None] == band_place[None, :]).astype(jnp.float32)
    band_sums = jnp.dot(band_select, near_terms, precision=lax.Precision.HIGHEST)
    band_sums = band_sums.reshape(3 * local_count, 2, full_width, leaf_size)
    extended = extended_2(band_sums, (("clus", 0),), local_count)
    own_rows = (
        band_sums[local_count : 2 * local_count]
        + extended[:local_count]
        + extended[4 * local_count :]
    )
    near_field = lax.psum_scatter(own_rows, "rhs", scatter_dimension=2, tiled=True)
    combined = far_field + near_field
    return (
        combined.transpose(1, 2, 0, 3)
        .reshape(2, narrow_width, local_count * leaf_size)
        .astype(jnp.bfloat16)
    )


def solution(mesh):
    return jax.shard_map(
        body,
        mesh=mesh,
        in_specs=(
            P(None, "rhs", "clus"),
            P("clus", None, None, None),
            P("clus", None, None, None),
            P("clus", "rhs", None, None),
            P("clus", "rhs"),
            P("clus"),
            P("clus", "rhs", None, None, None),
            P("clus", "rhs"),
        ),
        out_specs=P(None, "rhs", "clus"),
        check_vma=False,
    )
```

profile of v0, /device:TPU:0, one launch (start us, length us, event | category | flops | bytes accessed | tf_op | source)
XLA Modules:
  0.0 165.1 jit_solution(9417510357176201196)
XLA Ops:
  7.4 6.5 %all_gather.3 = bf16[2,32,512]{2,1,0:T(8,128)(2,1)S(1)} all-gather(bf16[2,8,512]{2,1,0:T(8,128)(2,1)} %param.8), channel_id=1, replica_groups=mesh['clus'=8,'rhs'=4] {'rhs'}, dimensions={1}, use_global_device_ids=true | all-gather | bytes 81920 | tf_op jit(solution)/shard_map/all_gather | solution.py:21
  13.9 0.0 copy-start.4
  14.0 0.5 fusion.2
  14.5 0.1 copy-done.4
  14.6 0.1 add.76
  14.8 0.1 reshape.183
  15.0 0.4 fusion.33
  15.3 0.1 fusion.35
  15.5 4.6 %collective-permute-start = (f32[2,2,32,256]{3,2,0,1:T(8,128)S(1)}, f32[2,2,32,256]{3,2,0,1:T(8,128)}, u32[]{:S(2)}, u32[]{:S(2)}) collective-permute-start(f32[2,2,32,256]{3,2,0,1:T(8,128)S(1)} %copy.45), channel_id=1, source_target_pairs={{0,4},{4,8},{8,12},{12,16},{16,20},{20,24},{24,28},{1,5},{5,9},{9,... | collective-permute-start | bytes 393224 | tf_op jit(solution)/shard_map/ppermute | solution.py:14
  20.1 0.7 copy.47
  20.8 1.3 collective-permute-start.1
  22.1 0.2 convolution_bitcast_fusion.2
  22.3 0.1 eq.43
  22.4 0.1 compare_convert_fusion
  22.5 0.2 convolution_bitcast_fusion
  22.7 0.2 slice_subtract_fusion
  23.0 0.2 reshape.180
  23.2 0.1 dot_general.25
  23.4 0.6 convolution_bitcast_fusion.1
  24.0 0.1 copy.38
  24.1 1.0 reshape.181
  25.1 0.0 all-reduce.3.cloned.1.call-update
  25.1 0.0 reduce-scatter.2.cloned.1.call-start
  25.2 3.2 %collective-permute-done.1 = f32[2,2,32,256]{3,2,0,1:T(8,128)} collective-permute-done((f32[2,2,32,256]{3,2,0,1:T(8,128)}, f32[2,2,32,256]{3,2,0,1:T(8,128)}, u32[]{:S(2)}, u32[]{:S(2)}) %collective-permute-start.1) | collective-permute-done | bytes 131104 | tf_op jit(solution)/shard_map/ppermute | solution.py:15
  28.4 1.7 %fusion.13 = f32[2,2,32,256]{3,2,0,1:T(8,128)} fusion(f32[2,2,32,256]{3,2,0,1:T(8,128)} %collective-permute-done.1, f32[2,2,32,256]{3,2,0,1:T(8,128)} %collective-permute-done, f32[2,2,32,256]{3,2,1,0:T(8,128)S(1)} %bitcast.121), kind=kLoop, calls=%fused_computation.23 | loop fusion | flops 65536 | bytes 524288 | tf_op jit(solution)/shard_map/add | solution.py:80
  30.1 0.0 reduce-scatter.2.cloned.1.call-update
  30.1 125.0 %all-reduce.3.cloned.1.call-done = f32[32,3072]{1,0:T(8,128)} async-done(((f32[32,3072]{1,0:T(8,128)}), f32[32,3072]{1,0:T(8,128)}) %all-reduce.3.cloned.1.call-update) | async-done | bytes 393232
  155.1 0.9 dynamic-slice_reduce_fusion
  156.1 0.1 reshape.182
  156.1 0.1 convolution_bitcast_fusion.3
  156.3 0.0 reduce-scatter.2.cloned.1.call-done
  156.3 1.4 fusion.21
  (31 shorter events, 0.3 us)
Async XLA Ops:
  7.4 6.6 %copy-start = (bf16[2,4,2,256,256]{4,3,2,1,0:T(8,128)(2,1)S(1)}, bf16[2,4,2,256,256]{4,3,2,1,0:T(8,128)(2,1)}, u32[]{:S(2)}) copy-start(bf16[2,4,2,256,256]{4,3,2,1,0:T(8,128)(2,1)} %param.14) | copy-start | bytes 6291460
  7.4 147.8 %all-reduce.3.cloned.1.call-start = ((), (), s32[]{:S(2)}) async-start(), calls=%async_computation.2 | async-start | bytes 786432
  13.9 0.7 copy-start.4
  14.8 7.5 %copy-start.5 = (s32[2,6]{1,0:T(2,128)S(1)}, s32[2,6]{1,0:T(2,128)}, u32[]{:S(2)}) copy-start(s32[2,6]{1,0:T(2,128)} %param.12) | copy-start | bytes 148
  14.8 7.6 %copy-start.6 = (s32[2]{0:T(128)S(1)}, s32[2]{0:T(128)}, u32[]{:S(2)}) copy-start(s32[2]{0:T(128)} %param.13) | copy-start | bytes 28
  14.9 7.1 %copy-start.2 = (bf16[2,2,96,256]{3,2,1,0:T(8,128)(2,1)S(1)}, bf16[2,2,96,256]{3,2,1,0:T(8,128)(2,1)}, u32[]{:S(2)}) copy-start(bf16[2,2,96,256]{3,2,1,0:T(8,128)(2,1)} %param.9) | copy-start | bytes 589828
  15.0 7.5 %copy-start.1 = (bf16[2,6,96,192]{3,2,1,0:T(8,128)(2,1)S(1)}, bf16[2,6,96,192]{3,2,1,0:T(8,128)(2,1)}, u32[]{:S(2)}) copy-start(bf16[2,6,96,192]{3,2,1,0:T(8,128)(2,1)} %param.11) | copy-start | bytes 1327108
  15.5 9.7 %collective-permute-start = (f32[2,2,32,256]{3,2,0,1:T(8,128)S(1)}, f32[2,2,32,256]{3,2,0,1:T(8,128)}, u32[]{:S(2)}, u32[]{:S(2)}) collective-permute-start(f32[2,2,32,256]{3,2,0,1:T(8,128)S(1)} %copy.45), channel_id=1, source_target_pairs={{0,4},{4,8},{8,12},{12,16},{16,20},{20,24},{24,28},{1,5},{5,9},{9,... | collective-permute-start | bytes 393224 | tf_op jit(solution)/shard_map/ppermute | solution.py:14
  20.8 7.7 %collective-permute-start.1 = (f32[2,2,32,256]{3,2,0,1:T(8,128)}, f32[2,2,32,256]{3,2,0,1:T(8,128)}, u32[]{:S(2)}, u32[]{:S(2)}) collective-permute-start(f32[2,2,32,256]{3,2,0,1:T(8,128)} %copy.47), channel_id=1, source_target_pairs={{4,0},{8,4},{12,8},{16,12},{20,16},{24,20},{28,24},{5,1},{9,5},{13... | collective-permute-start | bytes 393224 | tf_op jit(solution)/shard_map/ppermute | solution.py:15
  23.4 132.8 %copy-start.3 = (bf16[2,2,96,256]{3,2,1,0:T(8,128)(2,1)S(1)}, bf16[2,2,96,256]{3,2,1,0:T(8,128)(2,1)}, u32[]{:S(2)}) copy-start(bf16[2,2,96,256]{3,2,1,0:T(8,128)(2,1)} %param.10) | copy-start | bytes 589828
  25.1 131.2 %reduce-scatter.2.cloned.1.call-start = ((), (), s32[]{:S(2)}) async-start(), calls=%async_computation.1 | async-start | bytes 163840 | tf_op jit(solution)/shard_map/reduce_scatter | solution.py:84
Sparse Core Ops, SparseCore 0:
  25.3 129.8 all-reduce.2
Sparse Core Ops, SparseCore 1:
  30.2 20.1 reduce-scatter.1
where the time goes:
time: 165 us
  waiting for transfers between devices  128 us (78%)
  between operations  15.1 us (9%)
  blocking collectives  6.54 us (4%)
  starting transfers between devices  5.89 us (4%)
  local copies, waits for them, and re-layouts  3.85 us (2%)
  other arithmetic  3.44 us (2%)
  matrix products  2.02 us (1%)
    unnamed x3, waiting for transfers between devices  125 us
    all_gather x1, blocking collectives, body(): rhs_all = lax.all_gather(rhs_in, 'rhs', axis=1, tiled=True)  6.54 us
    ppermute x1, starting transfers between devices, extended_2(): before = lax.ppermute(last, axis, up)  4.56 us
  transfers between devices with their start and end apart: 4, of which 2 were waited for; matrix products, arithmetic and copies ran while one was open for 4% of the time, Pallas kernels for 0%

commit v1 on v0

v1 whole, which is shorter than its diff:
```python
import functools

import jax
import jax.numpy as jnp
from jax import lax
from jax.experimental import pallas as pl
from jax.experimental.pallas import tpu as pltpu
from jax.sharding import PartitionSpec as P

MESH = pl.DeviceIdType.MESH
F32 = jnp.float32
BF16 = jnp.bfloat16


def turned(v, half):
    parts = []
    for start in range(0, v.shape[0], 2 * half):
        parts.append(-v[start + half : start + 2 * half])
        parts.append(v[start : start + half])
    return jnp.concatenate(parts, axis=0)


def kernel(
    clus_n, rhs_n,
    rank_ref, fcol_ref, ncol_ref, x_ref, rb_hbm, cp_hbm, nb_hbm, cb_hbm,
    out_ref,
    rb, cp, nb, cb, xs, xr, terms, fsend, frecv, fown, fbs, fbr, prods, nsend, nrecv, nbs, nbr,
    load_sem, xs_sem, xr_sem, fs_sem, fr_sem, ns_sem, nr_sem, bs_sem, br_sem, ls_sem, lr_sem,
):
    me_c, me_r = lax.axis_index("clus"), lax.axis_index("rhs")
    half, leaf = x_ref.shape[1], nb.shape[3]
    rows = 2 * half
    local_n, near_n = nb.shape[0], nb.shape[1]
    far_n, rank_w = cp.shape[1], cp.shape[2]

    loads = [
        pltpu.make_async_copy(src, dst, load_sem.at[i])
        for i, (src, dst) in enumerate(((rb_hbm, rb), (cp_hbm, cp), (nb_hbm, nb), (cb_hbm, cb)))
    ]
    for load in loads:
        load.start()

    barrier = pltpu.get_barrier_semaphore()
    peers = [lax.rem(me_r + rhs_n - o, rhs_n) for o in range(rhs_n)]
    for o in range(1, rhs_n):
        pl.semaphore_signal(barrier, inc=1, device_id={"rhs": peers[o]}, device_id_type=MESH)

    def greet(o, carry):
        other = lax.rem(me_c + o, clus_n)
        pl.semaphore_signal(barrier, inc=1, device_id={"clus": other}, device_id_type=MESH)
        return carry

    lax.fori_loop(1, clus_n, greet, 0)
    xs[...] = jnp.concatenate([x_ref[0].astype(F32), x_ref[1].astype(F32)], axis=0).astype(BF16)

    @pl.when(me_c == 0)
    def _():
        nbr[0] = jnp.zeros_like(nbr[0])

    @pl.when(me_c == clus_n - 1)
    def _():
        nbr[1] = jnp.zeros_like(nbr[1])

    pl.semaphore_wait(barrier, rhs_n - 1 + clus_n - 1)

    def to_peer(src, dst, send, recv, o, forward=False):
        return pltpu.make_async_remote_copy(
            src_ref=src, dst_ref=dst.at[o - 1], send_sem=send.at[o - 1], recv_sem=recv.at[o - 1],
            device_id={"rhs": lax.rem(me_r + o, rhs_n) if forward else peers[o]}, device_id_type=MESH,
        )

    x_copies = [to_peer(xs, xr, xs_sem, xr_sem, o, forward=True) for o in range(1, rhs_n)]
    for copy in x_copies:
        copy.start()
    loads[0].wait()
    loads[1].wait()
    for copy in x_copies:
        copy.wait()

    fields = []
    for c in range(local_n):
        cols = slice(c * leaf, (c + 1) * leaf)
        plain = jnp.concatenate([xs[:, cols]] + [xr[o, :, cols] for o in range(rhs_n - 1)], axis=0)
        fields.append((plain, turned(plain.astype(F32), half).astype(BF16)))

    lanes = lax.broadcasted_iota(jnp.int32, (rhs_n * rows, rank_w), 1)
    last = (((1,), (1,)), ((), ()))
    for c in range(local_n):
        coeff = lax.dot_general(
            fields[c][0], rb[c, :rank_w], last, preferred_element_type=F32
        ) + lax.dot_general(fields[c][1], rb[c, rank_w:], last, preferred_element_type=F32)
        coeff = jnp.where(lanes < rank_ref[c], coeff, 0.0).astype(BF16)
        for f in range(far_n):
            coupled = jnp.dot(coeff, cp[c, f], preferred_element_type=F32)
            terms[c * far_n + f] = coupled[:, :rank_w] + turned(coupled[:, rank_w:], half)

    def spread(g, carry):
        for l in range(local_n):
            total = None
            for b in range(local_n * far_n):
                here = fcol_ref[b // far_n, b % far_n] == g * local_n + l
                part = terms[b] * jnp.where(here, 1.0, 0.0)
                total = part if total is None else total + part
            for o in range(rhs_n):
                fsend[o, g, l] = total[o * rows : (o + 1) * rows].astype(BF16)
        return carry

    lax.fori_loop(0, clus_n, spread, 0)
    f_copies = [to_peer(fsend.at[o], frecv, fs_sem, fr_sem, o) for o in range(1, rhs_n)]
    for copy in f_copies:
        copy.start()

    loads[2].wait()
    for c in range(local_n):
        both = jnp.concatenate(fields[c], axis=1)
        for n in range(near_n):
            prods[c * near_n + n] = jnp.dot(both, nb[c, n], preferred_element_type=F32)
    for d in range(3):
        for l in range(local_n):
            place = (d - 1) * local_n + l
            total = None
            for c in range(local_n):
                if abs(place - c) > 2:
                    continue
                for n in range(near_n):
                    here = ncol_ref[c, n] - me_c * local_n == place
                    part = prods[c * near_n + n] * jnp.where(here, 1.0, 0.0)
                    total = part if total is None else total + part
            for o in range(rhs_n):
                nsend[o, d, l] = total[o * rows : (o + 1) * rows].astype(BF16)
    n_copies = [to_peer(nsend.at[o], nrecv, ns_sem, nr_sem, o) for o in range(1, rhs_n)]
    for copy in n_copies:
        copy.start()

    for copy in f_copies:
        copy.wait_recv()

    def far_here(g):
        total = fsend[0, g].astype(F32)
        for o in range(rhs_n - 1):
            total += frecv[o, g].astype(F32)
        return total

    def far_copy(o):
        return pltpu.make_async_remote_copy(
            src_ref=fbs.at[o - 1], dst_ref=fbr.at[o - 1],
            send_sem=bs_sem.at[o - 1], recv_sem=br_sem.at[o - 1],
            device_id={"clus": lax.rem(me_c + o, clus_n)}, device_id_type=MESH,
        )

    def far_out(o, carry):
        fbs[o - 1] = far_here(lax.rem(me_c + o, clus_n)).astype(BF16)
        far_copy(o).start()
        return carry

    lax.fori_loop(1, clus_n, far_out, 0)
    fown[...] = far_here(me_c)

    for copy in n_copies:
        copy.wait_recv()

    def near_here(d):
        total = nsend[0, d].astype(F32)
        for o in range(rhs_n - 1):
            total += nrecv[o, d].astype(F32)
        return total

    def near_copy(side):
        other = me_c - 1 if side == 0 else me_c + 1
        return pltpu.make_async_remote_copy(
            src_ref=nbs.at[side], dst_ref=nbr.at[1 - side],
            send_sem=ls_sem.at[side], recv_sem=lr_sem.at[1 - side],
            device_id={"clus": other}, device_id_type=MESH,
        )

    nbs[0] = near_here(0).astype(BF16)

    @pl.when(me_c > 0)
    def _():
        near_copy(0).start()

    nbs[1] = near_here(2).astype(BF16)

    @pl.when(me_c < clus_n - 1)
    def _():
        near_copy(1).start()

    near_own = near_here(1)
    loads[3].wait()

    def far_in(o, total):
        far_copy(o).wait_recv()
        return total + fbr[o - 1].astype(F32)

    far_sum = lax.fori_loop(1, clus_n, far_in, fown[...])
    lanes = lax.broadcasted_iota(jnp.int32, (rows, rank_w), 1)
    far_fields = []
    for l in range(local_n):
        coeff = jnp.where(lanes < rank_ref[l], far_sum[l], 0.0).astype(BF16)
        swapped = turned(coeff.astype(F32), half).astype(BF16)
        far_fields.append(
            jnp.dot(coeff, cb[l, :rank_w], preferred_element_type=F32)
            + jnp.dot(swapped, cb[l, rank_w:], preferred_element_type=F32)
        )

    @pl.when(me_c > 0)
    def _():
        near_copy(1).wait_recv()

    @pl.when(me_c < clus_n - 1)
    def _():
        near_copy(0).wait_recv()

    for l in range(local_n):
        field = far_fields[l] + near_own[l] + nbr[0, l].astype(F32) + nbr[1, l].astype(F32)
        for p in range(2):
            out_ref[p, :, l * leaf : (l + 1) * leaf] = field[p * half : (p + 1) * half].astype(BF16)

    for copy in f_copies + n_copies:
        copy.wait_send()

    def far_sent(o, carry):
        far_copy(o).wait_send()
        return carry

    lax.fori_loop(1, clus_n, far_sent, 0)

    @pl.when(me_c > 0)
    def _():
        near_copy(0).wait_send()

    @pl.when(me_c < clus_n - 1)
    def _():
        near_copy(1).wait_send()


def body(clus_n, rhs_n, rhs_in, row_basis, col_basis, coupling, far_col, cluster_rank, near_block, near_col):
    _, half, width = rhs_in.shape
    local_n, _, rank_w, leaf = row_basis.shape
    far_n, near_n = coupling.shape[1], near_block.shape[1]
    rows = 2 * half
    rb = row_basis.reshape(local_n, 2 * rank_w, leaf)
    cb = col_basis.reshape(local_n, 2 * rank_w, leaf)
    nb = near_block.reshape(local_n, near_n, 2 * leaf, leaf)
    others, away = rhs_n - 1, clus_n - 1
    dma = pltpu.SemaphoreType.DMA
    smem = pl.BlockSpec(memory_space=pltpu.SMEM)
    vmem = pl.BlockSpec(memory_space=pltpu.VMEM)
    hbm = pl.BlockSpec(memory_space=pl.ANY)
    return pl.pallas_call(
        functools.partial(kernel, clus_n, rhs_n),
        out_shape=jax.ShapeDtypeStruct(rhs_in.shape, BF16),
        in_specs=[smem] * 3 + [vmem] + [hbm] * 4,
        out_specs=vmem,
        scratch_shapes=[
            pltpu.VMEM(rb.shape, BF16),
            pltpu.VMEM(coupling.shape, BF16),
            pltpu.VMEM(nb.shape, BF16),
            pltpu.VMEM(cb.shape, BF16),
            pltpu.VMEM((rows, width), BF16),
            pltpu.VMEM((others, rows, width), BF16),
            pltpu.VMEM((local_n * far_n, rhs_n * rows, rank_w), F32),
            pltpu.VMEM((rhs_n, clus_n, local_n, rows, rank_w), BF16),
            pltpu.VMEM((others, clus_n, local_n, rows, rank_w), BF16),
            pltpu.VMEM((local_n, rows, rank_w), F32),
            pltpu.VMEM((away, local_n, rows, rank_w), BF16),
            pltpu.VMEM((away, local_n, rows, rank_w), BF16),
            pltpu.VMEM((local_n * near_n, rhs_n * rows, leaf), F32),
            pltpu.VMEM((rhs_n, 3, local_n, rows, leaf), BF16),
            pltpu.VMEM((others, 3, local_n, rows, leaf), BF16),
            pltpu.VMEM((2, local_n, rows, leaf), BF16),
            pltpu.VMEM((2, local_n, rows, leaf), BF16),
            dma((4,)),
            dma((others,)),
            dma((others,)),
            dma((others,)),
            dma((others,)),
            dma((others,)),
            dma((others,)),
            dma((away,)),
            dma((away,)),
            dma((2,)),
            dma((2,)),
        ],
        compiler_params=pltpu.CompilerParams(
            collective_id=0, has_side_effects=True, vmem_limit_bytes=40 * 2**20
        ),
    )(cluster_rank, far_col, near_col, rhs_in, rb, coupling, nb, cb)


def solution(mesh):
    return jax.shard_map(
        functools.partial(body, mesh.shape["clus"], mesh.shape["rhs"]),
        mesh=mesh,
        in_specs=(
            P(None, "rhs", "clus"),
            P("clus", None, None, None),
            P("clus", None, None, None),
            P("clus", "rhs", None, None),
            P("clus", "rhs"),
            P("clus"),
            P("clus", "rhs", None, None, None),
            P("clus", "rhs"),
        ),
        out_specs=P(None, "rhs", "clus"),
        check_vma=False,
    )
```

time: 165 us -> 29.1 us (0.18)
  waiting for transfers between devices: 128 us -> 0 us
  Pallas kernels: 0 us -> 20.9 us
  between operations: 15.1 us -> 0.02 us
  blocking collectives: 6.54 us -> 0 us
  starting transfers between devices: 5.89 us -> 0 us
  local copies, waits for them, and re-layouts: 3.85 us -> 7.84 us
  other arithmetic: 3.44 us -> 0 us
  matrix products: 2.02 us -> 0 us
    unnamed x3 -> x0, waiting for transfers between devices: 125 us -> none
    pallas_call x0 -> x1, Pallas kernels: none -> 20.9 us  [body(): pl.pallas_call(functools.partial(kernel, clus_n, rhs_n), out_shape=jax.Sh...]
    unnamed x18 -> x17, local copies, waits for them, and re-layouts: 1.09 us -> 7.84 us
    all_gather x1 -> x0, blocking collectives: 6.54 us -> none  [body(): rhs_all = lax.all_gather(rhs_in, 'rhs', axis=1, tiled=True)]
    ppermute x2 -> x0, starting transfers between devices: 5.84 us -> none  [the longest x1 4.56 us: extended_2(): before = lax.ppermute(last, axis, up)]
    ppermute x2 -> x0, waiting for transfers between devices: 3.18 us -> none  [the longest x1 3.18 us: extended_2(): after = lax.ppermute(first, axis, down)]
    dot_general x6 -> x0, matrix products: 2.02 us -> none  [the longest x1 0.6 us: body(): jnp.dot(far_select, far_terms, precision=lax.Precision.HIGHEST)]
    add x5 -> x0, other arithmetic: 1.71 us -> none  [the longest x1 1.65 us: body(): band_sums[local_count:2 * local_count] + extended[:local_count]]
  transfers between devices with their start and end apart: 4 -> 0, of which waited for: 2 -> 0; matrix products, arithmetic and copies ran while one was open for 4% -> 0% of each run, Pallas kernels for 0% -> 0%
where the time goes in v1:
time: 29.1 us; the launch traced here: 28.8 us
  Pallas kernels  20.9 us (72%)
  local copies, waits for them, and re-layouts  7.84 us (27%)
    pallas_call x1, Pallas kernels, body(): pl.pallas_call(functools.partial(kernel, clus_n, rhs_n), out_shape=jax.Sh...  20.9 us
    unnamed x17, local copies, waits for them, and re-layouts  7.84 us

profile of v1, /device:TPU:0, one launch (start us, length us, event | category | flops | bytes accessed | tf_op | source)
XLA Modules:
  0.0 28.8 jit_solution(3696471134288095414)
XLA Ops:
  0.0 0.0 copy-start
  0.0 1.6 %copy-done = bf16[2,4,2,256,256]{4,3,2,1,0:T(8,128)(2,1)S(1)} copy-done((bf16[2,4,2,256,256]{4,3,2,1,0:T(8,128)(2,1)S(1)}, bf16[2,4,2,256,256]{4,3,2,1,0:T(8,128)(2,1)}, u32[]{:S(2)}) %copy-start) | copy-done | bytes 2097176
  1.6 0.0 copy-start.1
  1.6 1.1 %copy-done.1 = bf16[2,6,96,192]{3,2,1,0:T(8,128)(2,1)S(1)} copy-done((bf16[2,6,96,192]{3,2,1,0:T(8,128)(2,1)S(1)}, bf16[2,6,96,192]{3,2,1,0:T(8,128)(2,1)}, u32[]{:S(2)}) %copy-start.1) | copy-done | bytes 442392
  2.7 0.0 copy-start.2
  2.7 0.9 %copy-done.2 = bf16[2,2,96,256]{3,2,1,0:T(8,128)(2,1)S(1)} copy-done((bf16[2,2,96,256]{3,2,1,0:T(8,128)(2,1)S(1)}, bf16[2,2,96,256]{3,2,1,0:T(8,128)(2,1)}, u32[]{:S(2)}) %copy-start.2) | copy-done | bytes 196632
  3.6 0.0 copy-start.3
  3.6 0.9 %copy-done.3 = bf16[2,2,96,256]{3,2,1,0:T(8,128)(2,1)S(1)} copy-done((bf16[2,2,96,256]{3,2,1,0:T(8,128)(2,1)S(1)}, bf16[2,2,96,256]{3,2,1,0:T(8,128)(2,1)}, u32[]{:S(2)}) %copy-start.3) | copy-done | bytes 196632
  4.5 0.0 copy-start.4
  4.5 0.7 %copy-done.4 = bf16[2,8,512]{2,1,0:T(8,128)(2,1)S(1)} copy-done((bf16[2,8,512]{2,1,0:T(8,128)(2,1)S(1)}, bf16[2,8,512]{2,1,0:T(8,128)(2,1)}, u32[]{:S(2)}) %copy-start.4) | copy-done | bytes 16408
  5.2 0.0 copy-start.5
  5.2 0.7 %copy-done.5 = s32[2,6]{1,0:T(2,128)S(1)} copy-done((s32[2,6]{1,0:T(2,128)S(1)}, s32[2,6]{1,0:T(2,128)}, u32[]{:S(2)}) %copy-start.5) | copy-done | bytes 72
  5.9 0.0 copy-start.6
  5.9 0.7 %copy-done.6 = s32[2,4]{1,0:T(2,128)S(1)} copy-done((s32[2,4]{1,0:T(2,128)S(1)}, s32[2,4]{1,0:T(2,128)}, u32[]{:S(2)}) %copy-start.6) | copy-done | bytes 56
  6.6 0.0 copy-start.7
  6.6 0.7 %copy-done.7 = s32[2]{0:T(128)S(1)} copy-done((s32[2]{0:T(128)S(1)}, s32[2]{0:T(128)}, u32[]{:S(2)}) %copy-start.7) | copy-done | bytes 32
  7.2 20.9 %shard_map.82 = bf16[2,8,512]{2,1,0:T(8,128)(2,1)S(1)} custom-call(s32[2]{0:T(128)S(1)} %copy-done.7, s32[2,6]{1,0:T(2,128)S(1)} %copy-done.5, s32[2,4]{1,0:T(2,128)S(1)} %copy-done.6, bf16[2,8,512]{2,1,0:T(8,128)(2,1)S(1)} %copy-done.4, bf16[2,192,256]{2,1,0:T(8,128)(2,1)S(1)} %bitcast.4, bf16[2,6,96,192]{3,2,1,0:T(8,128)(2,1)S(1)} %copy-done.1, ...), custom_call_target="tpu_custom_call" | custom-call | tf_op jit(solution)/shard_map/pallas_call | solution.py:250
  28.1 0.6 %copy.10 = bf16[2,8,512]{2,1,0:T(8,128)(2,1)} copy(bf16[2,8,512]{2,1,0:T(8,128)(2,1)S(1)} %shard_map.82) | data formatting | bytes 32768
Async XLA Ops:
  0.0 1.6 %copy-start = (bf16[2,4,2,256,256]{4,3,2,1,0:T(8,128)(2,1)S(1)}, bf16[2,4,2,256,256]{4,3,2,1,0:T(8,128)(2,1)}, u32[]{:S(2)}) copy-start(bf16[2,4,2,256,256]{4,3,2,1,0:T(8,128)(2,1)} %param.14) | copy-start | bytes 6291460
  1.6 1.1 %copy-start.1 = (bf16[2,6,96,192]{3,2,1,0:T(8,128)(2,1)S(1)}, bf16[2,6,96,192]{3,2,1,0:T(8,128)(2,1)}, u32[]{:S(2)}) copy-start(bf16[2,6,96,192]{3,2,1,0:T(8,128)(2,1)} %cp_hbm.1) | copy-start | bytes 1327108
  2.7 0.9 %copy-start.2 = (bf16[2,2,96,256]{3,2,1,0:T(8,128)(2,1)S(1)}, bf16[2,2,96,256]{3,2,1,0:T(8,128)(2,1)}, u32[]{:S(2)}) copy-start(bf16[2,2,96,256]{3,2,1,0:T(8,128)(2,1)} %param.9) | copy-start | bytes 589828
  3.6 0.9 %copy-start.3 = (bf16[2,2,96,256]{3,2,1,0:T(8,128)(2,1)S(1)}, bf16[2,2,96,256]{3,2,1,0:T(8,128)(2,1)}, u32[]{:S(2)}) copy-start(bf16[2,2,96,256]{3,2,1,0:T(8,128)(2,1)} %param.10) | copy-start | bytes 589828
  4.5 0.7 %copy-start.4 = (bf16[2,8,512]{2,1,0:T(8,128)(2,1)S(1)}, bf16[2,8,512]{2,1,0:T(8,128)(2,1)}, u32[]{:S(2)}) copy-start(bf16[2,8,512]{2,1,0:T(8,128)(2,1)} %x_ref.1) | copy-start | bytes 49156
  5.2 0.7 %copy-start.5 = (s32[2,6]{1,0:T(2,128)S(1)}, s32[2,6]{1,0:T(2,128)}, u32[]{:S(2)}) copy-start(s32[2,6]{1,0:T(2,128)} %fcol_ref.1) | copy-start | bytes 148
  5.9 0.7 %copy-start.6 = (s32[2,4]{1,0:T(2,128)S(1)}, s32[2,4]{1,0:T(2,128)}, u32[]{:S(2)}) copy-start(s32[2,4]{1,0:T(2,128)} %ncol_ref.1) | copy-start | bytes 100
  6.6 0.7 %copy-start.7 = (s32[2]{0:T(128)S(1)}, s32[2]{0:T(128)}, u32[]{:S(2)}) copy-start(s32[2]{0:T(128)} %rank_ref.1) | copy-start | bytes 28

commit v2 on v1

--- a/solution.py
+++ b/solution.py
@@ -24,7 +24,7 @@
     clus_n, rhs_n,
     rank_ref, fcol_ref, ncol_ref, x_ref, rb_hbm, cp_hbm, nb_hbm, cb_hbm,
     out_ref,
-    rb, cp, nb, cb, xs, xr, terms, fsend, frecv, fown, fbs, fbr, prods, nsend, nrecv, nbs, nbr,
+    rb, cp, nb, cb, xs, xr, terms, fsend, frecv, fown, fbs, fbr, prods, nown, nsend, nrecv, nbs, nbr,
     load_sem, xs_sem, xr_sem, fs_sem, fr_sem, ns_sem, nr_sem, bs_sem, br_sem, ls_sem, lr_sem,
 ):
     me_c, me_r = lax.axis_index("clus"), lax.axis_index("rhs")
@@ -126,44 +126,10 @@
                     here = ncol_ref[c, n] - me_c * local_n == place
                     part = prods[c * near_n + n] * jnp.where(here, 1.0, 0.0)
                     total = part if total is None else total + part
-            for o in range(rhs_n):
-                nsend[o, d, l] = total[o * rows : (o + 1) * rows].astype(BF16)
-    n_copies = [to_peer(nsend.at[o], nrecv, ns_sem, nr_sem, o) for o in range(1, rhs_n)]
-    for copy in n_copies:
-        copy.start()
-
-    for copy in f_copies:
-        copy.wait_recv()
-
-    def far_here(g):
-        total = fsend[0, g].astype(F32)
-        for o in range(rhs_n - 1):
-            total += frecv[o, g].astype(F32)
-        return total
-
-    def far_copy(o):
-        return pltpu.make_async_remote_copy(
-            src_ref=fbs.at[o - 1], dst_ref=fbr.at[o - 1],
-            send_sem=bs_sem.at[o - 1], recv_sem=br_sem.at[o - 1],
-            device_id={"clus": lax.rem(me_c + o, clus_n)}, device_id_type=MESH,
-        )
-
-    def far_out(o, carry):
-        fbs[o - 1] = far_here(lax.rem(me_c + o, clus_n)).astype(BF16)
-        far_copy(o).start()
-        return carry
-
-    lax.fori_loop(1, clus_n, far_out, 0)
-    fown[...] = far_here(me_c)
-
-    for copy in n_copies:
-        copy.wait_recv()
-
-    def near_here(d):
-        total = nsend[0, d].astype(F32)
-        for o in range(rhs_n - 1):
-            total += nrecv[o, d].astype(F32)
-        return total
+            if d == 1:
+                nown[l] = total
+            else:
+                nbs[d // 2, l] = total.astype(BF16)
 
     def near_copy(side):
         other = me_c - 1 if side == 0 else me_c + 1
@@ -173,19 +139,56 @@
             device_id={"clus": other}, device_id_type=MESH,
         )
 
-    nbs[0] = near_here(0).astype(BF16)
-
     @pl.when(me_c > 0)
     def _():
         near_copy(0).start()
 
-    nbs[1] = near_here(2).astype(BF16)
-
     @pl.when(me_c < clus_n - 1)
     def _():
         near_copy(1).start()
 
-    near_own = near_here(1)
+    for copy in f_copies:
+        copy.wait_recv()
+
+    def far_here(g):
+        total = fsend[0, g].astype(F32)
+        for o in range(rhs_n - 1):
+            total += frecv[o, g].astype(F32)
+        return total
+
+    def far_copy(o):
+        return pltpu.make_async_remote_copy(
+            src_ref=fbs.at[o - 1], dst_ref=fbr.at[o - 1],
+            send_sem=bs_sem.at[o - 1], recv_sem=br_sem.at[o - 1],
+            device_id={"clus": lax.rem(me_c + o, clus_n)}, device_id_type=MESH,
+        )
+
+    def far_out(o, carry):
+        fbs[o - 1] = far_here(lax.rem(me_c + o, clus_n)).astype(BF16)
+        far_copy(o).start()
+        return carry
+
+    lax.fori_loop(1, clus_n, far_out, 0)
+    fown[...] = far_here(me_c)
+
+    @pl.when(me_c > 0)
+    def _():
+        near_copy(1).wait_recv()
+
+    @pl.when(me_c < clus_n - 1)
+    def _():
+        near_copy(0).wait_recv()
+
+    near_own = []
+    for l in range(local_n):
+        total = nown[l] + nbr[0, l].astype(F32) + nbr[1, l].astype(F32)
+        near_own.append(total[:rows])
+        for o in range(1, rhs_n):
+            nsend[o - 1, l] = total[o * rows : (o + 1) * rows].astype(BF16)
+    n_copies = [to_peer(nsend.at[o - 1], nrecv, ns_sem, nr_sem, o) for o in range(1, rhs_n)]
+    for copy in n_copies:
+        copy.start()
+
     loads[3].wait()
 
     def far_in(o, total):
@@ -203,16 +206,12 @@
             + jnp.dot(swapped, cb[l, rank_w:], preferred_element_type=F32)
         )
 
-    @pl.when(me_c > 0)
-    def _():
-        near_copy(1).wait_recv()
-
-    @pl.when(me_c < clus_n - 1)
-    def _():
-        near_copy(0).wait_recv()
-
+    for copy in n_copies:
+        copy.wait_recv()
     for l in range(local_n):
-        field = far_fields[l] + near_own[l] + nbr[0, l].astype(F32) + nbr[1, l].astype(F32)
+        field = far_fields[l] + near_own[l]
+        for o in range(rhs_n - 1):
+            field += nrecv[o, l].astype(F32)
         for p in range(2):
             out_ref[p, :, l * leaf : (l + 1) * leaf] = field[p * half : (p + 1) * half].astype(BF16)
 
@@ -266,10 +265,11 @@
             pltpu.VMEM((away, local_n, rows, rank_w), BF16),
             pltpu.VMEM((away, local_n, rows, rank_w), BF16),
             pltpu.VMEM((local_n * near_n, rhs_n * rows, leaf), F32),
-            pltpu.VMEM((rhs_n, 3, local_n, rows, leaf), BF16),
-            pltpu.VMEM((others, 3, local_n, rows, leaf), BF16),
-            pltpu.VMEM((2, local_n, rows, leaf), BF16),
-            pltpu.VMEM((2, local_n, rows, leaf), BF16),
+            pltpu.VMEM((local_n, rhs_n * rows, leaf), F32),
+            pltpu.VMEM((others, local_n, rows, leaf), BF16),
+            pltpu.VMEM((others, local_n, rows, leaf), BF16),
+            pltpu.VMEM((2, local_n, rhs_n * rows, leaf), BF16),
+            pltpu.VMEM((2, local_n, rhs_n * rows, leaf), BF16),
             dma((4,)),
             dma((others,)),
             dma((others,)),
@@ -283,7 +283,7 @@
             dma((2,)),
         ],
         compiler_params=pltpu.CompilerParams(
-            collective_id=0, has_side_effects=True, vmem_limit_bytes=40 * 2**20
+            collective_id=0, has_side_effects=True, vmem_limit_bytes=63 * 2**20
         ),
     )(cluster_rank, far_col, near_col, rhs_in, rb, coupling, nb, cb)
 

time: 29.1 us -> 21.6 us (0.74)
  local copies, waits for them, and re-layouts: 7.84 us -> 1.32 us
  Pallas kernels: 20.9 us -> 20 us
    unnamed x17 -> x1, local copies, waits for them, and re-layouts: 7.84 us -> 1.32 us
    pallas_call x1, Pallas kernels: 20.9 us -> 20 us  [body(): pl.pallas_call(functools.partial(kernel, clus_n, rhs_n), out_shape=jax.Sh...]
where the time goes in v2:
time: 21.6 us; the launch traced here: 21.3 us
  Pallas kernels  20 us (93%)
  local copies, waits for them, and re-layouts  1.32 us (6%)
    pallas_call x1, Pallas kernels, body(): pl.pallas_call(functools.partial(kernel, clus_n, rhs_n), out_shape=jax.Sh...  20 us
    unnamed x1, local copies, waits for them, and re-layouts  1.32 us

profile of v2, /device:TPU:0, one launch (start us, length us, event | category | flops | bytes accessed | tf_op | source)
XLA Modules:
  0.0 21.3 jit_solution(4327230409129464031)
XLA Ops:
  0.0 20.0 %shard_map.82 = bf16[2,8,512]{2,1,0:T(8,128)(2,1)} custom-call(s32[2]{0:T(128)} %rank_ref.1, s32[2,6]{1,0:T(2,128)} %fcol_ref.1, s32[2,4]{1,0:T(2,128)} %ncol_ref.1, bf16[2,8,512]{2,1,0:T(8,128)(2,1)} %x_ref.1, bf16[2,192,256]{2,1,0:T(8,128)(2,1)} %bitcast.4, bf16[2,6,96,192]{3,2,1,0:T(8,128)(2,1)} %cp_hbm.1, bf16[2,4,512,256]{3,2,1,0:T(8,128)(2,1)} %bitcast.3, ...), custom_call_target="tpu_custom_call" | custom-call | tf_op jit(solution)/shard_map/pallas_call | solution.py:249
  20.0 1.3 %copy.10 = bf16[2,8,512]{2,1,0:T(8,128)(2,1)} copy(bf16[2,8,512]{2,1,0:T(8,128)(2,1)} %shard_map.82) | data formatting | bytes 32768

commit v3 on v2

--- a/solution.py
+++ b/solution.py
@@ -1,4 +1,5 @@
 import functools
+import math
 
 import jax
 import jax.numpy as jnp
@@ -24,7 +25,7 @@
     clus_n, rhs_n,
     rank_ref, fcol_ref, ncol_ref, x_ref, rb_hbm, cp_hbm, nb_hbm, cb_hbm,
     out_ref,
-    rb, cp, nb, cb, xs, xr, terms, fsend, frecv, fown, fbs, fbr, prods, nown, nsend, nrecv, nbs, nbr,
+    rb, cp, nb, cb, xs, xr, terms, fsend, frecv, fbs, fbr, prods, nown, nsend, nrecv, nbs, nbr,
     load_sem, xs_sem, xr_sem, fs_sem, fr_sem, ns_sem, nr_sem, bs_sem, br_sem, ls_sem, lr_sem,
 ):
     me_c, me_r = lax.axis_index("clus"), lax.axis_index("rhs")
@@ -94,21 +95,33 @@
             coupled = jnp.dot(coeff, cp[c, f], preferred_element_type=F32)
             terms[c * far_n + f] = coupled[:, :rank_w] + turned(coupled[:, rank_w:], half)
 
-    def spread(g, carry):
-        for l in range(local_n):
+    packs = fsend.shape[1]
+    pack_n = fsend.shape[3] // rank_w
+
+    def far_part(o, h):
+        return pltpu.make_async_remote_copy(
+            src_ref=fsend.at[o, h], dst_ref=frecv.at[o - 1, h],
+            send_sem=fs_sem.at[o - 1, h], recv_sem=fr_sem.at[o - 1, h],
+            device_id={"rhs": peers[o]}, device_id_type=MESH,
+        )
+
+    def spread(h, carry):
+        totals = []
+        for j in range(pack_n):
             total = None
             for b in range(local_n * far_n):
-                here = fcol_ref[b // far_n, b % far_n] == g * local_n + l
+                here = fcol_ref[b // far_n, b % far_n] == h * pack_n + j
                 part = terms[b] * jnp.where(here, 1.0, 0.0)
                 total = part if total is None else total + part
-            for o in range(rhs_n):
-                fsend[o, g, l] = total[o * rows : (o + 1) * rows].astype(BF16)
-        return carry
-
-    lax.fori_loop(0, clus_n, spread, 0)
-    f_copies = [to_peer(fsend.at[o], frecv, fs_sem, fr_sem, o) for o in range(1, rhs_n)]
-    for copy in f_copies:
-        copy.start()
+            totals.append(total)
+        packed = jnp.concatenate(totals, axis=1)
+        for o in range(rhs_n):
+            fsend[o, h] = packed[o * rows : (o + 1) * rows].astype(BF16)
+            if o:
+                far_part(o, h).start()
+        return carry
+
+    lax.fori_loop(0, packs, spread, 0)
 
     loads[2].wait()
     for c in range(local_n):
@@ -147,29 +160,31 @@
     def _():
         near_copy(1).start()
 
-    for copy in f_copies:
-        copy.wait_recv()
-
-    def far_here(g):
-        total = fsend[0, g].astype(F32)
-        for o in range(rhs_n - 1):
-            total += frecv[o, g].astype(F32)
-        return total
-
-    def far_copy(o):
+    def far_copy(g, slot):
         return pltpu.make_async_remote_copy(
-            src_ref=fbs.at[o - 1], dst_ref=fbr.at[o - 1],
-            send_sem=bs_sem.at[o - 1], recv_sem=br_sem.at[o - 1],
-            device_id={"clus": lax.rem(me_c + o, clus_n)}, device_id_type=MESH,
-        )
-
-    def far_out(o, carry):
-        fbs[o - 1] = far_here(lax.rem(me_c + o, clus_n)).astype(BF16)
-        far_copy(o).start()
-        return carry
-
-    lax.fori_loop(1, clus_n, far_out, 0)
-    fown[...] = far_here(me_c)
+            src_ref=fbs.at[g], dst_ref=fbr.at[slot],
+            send_sem=bs_sem.at[g], recv_sem=br_sem.at[slot],
+            device_id={"clus": g}, device_id_type=MESH,
+        )
+
+    def far_out(h, carry):
+        total = fsend[0, h].astype(F32)
+        for o in range(1, rhs_n):
+            far_part(o, h).wait_recv()
+            total += frecv[o - 1, h].astype(F32)
+        for i in range(pack_n // local_n):
+            g = h * (pack_n // local_n) + i
+            for l in range(local_n):
+                j = i * local_n + l
+                fbs[g, l] = total[:, j * rank_w : (j + 1) * rank_w].astype(BF16)
+
+            @pl.when(g != me_c)
+            def _():
+                far_copy(g, me_c).start()
+
+        return carry
+
+    lax.fori_loop(0, packs, far_out, 0)
 
     @pl.when(me_c > 0)
     def _():
@@ -192,10 +207,11 @@
     loads[3].wait()
 
     def far_in(o, total):
-        far_copy(o).wait_recv()
-        return total + fbr[o - 1].astype(F32)
-
-    far_sum = lax.fori_loop(1, clus_n, far_in, fown[...])
+        slot = lax.rem(me_c + o, clus_n)
+        far_copy(slot, slot).wait_recv()
+        return total + fbr[slot].astype(F32)
+
+    far_sum = lax.fori_loop(1, clus_n, far_in, fbs[me_c].astype(F32))
     lanes = lax.broadcasted_iota(jnp.int32, (rows, rank_w), 1)
     far_fields = []
     for l in range(local_n):
@@ -215,11 +231,19 @@
         for p in range(2):
             out_ref[p, :, l * leaf : (l + 1) * leaf] = field[p * half : (p + 1) * half].astype(BF16)
 
-    for copy in f_copies + n_copies:
+    for copy in n_copies:
         copy.wait_send()
 
+    def parts_sent(h, carry):
+        for o in range(1, rhs_n):
+            far_part(o, h).wait_send()
+        return carry
+
+    lax.fori_loop(0, packs, parts_sent, 0)
+
     def far_sent(o, carry):
-        far_copy(o).wait_send()
+        slot = lax.rem(me_c + o, clus_n)
+        far_copy(slot, slot).wait_send()
         return carry
 
     lax.fori_loop(1, clus_n, far_sent, 0)
@@ -241,7 +265,9 @@
     rb = row_basis.reshape(local_n, 2 * rank_w, leaf)
     cb = col_basis.reshape(local_n, 2 * rank_w, leaf)
     nb = near_block.reshape(local_n, near_n, 2 * leaf, leaf)
-    others, away = rhs_n - 1, clus_n - 1
+    others = rhs_n - 1
+    pack_n = math.lcm(128 // math.gcd(rank_w, 128), local_n)
+    packs = clus_n * local_n // pack_n
     dma = pltpu.SemaphoreType.DMA
     smem = pl.BlockSpec(memory_space=pltpu.SMEM)
     vmem = pl.BlockSpec(memory_space=pltpu.VMEM)
@@ -259,11 +285,10 @@
             pltpu.VMEM((rows, width), BF16),
             pltpu.VMEM((others, rows, width), BF16),
             pltpu.VMEM((local_n * far_n, rhs_n * rows, rank_w), F32),
-            pltpu.VMEM((rhs_n, clus_n, local_n, rows, rank_w), BF16),
-            pltpu.VMEM((others, clus_n, local_n, rows, rank_w), BF16),
-            pltpu.VMEM((local_n, rows, rank_w), F32),
-            pltpu.VMEM((away, local_n, rows, rank_w), BF16),
-            pltpu.VMEM((away, local_n, rows, rank_w), BF16),
+            pltpu.VMEM((rhs_n, packs, rows, pack_n * rank_w), BF16),
+            pltpu.VMEM((others, packs, rows, pack_n * rank_w), BF16),
+            pltpu.VMEM((clus_n, local_n, rows, rank_w), BF16),
+            pltpu.VMEM((clus_n, local_n, rows, rank_w), BF16),
             pltpu.VMEM((local_n * near_n, rhs_n * rows, leaf), F32),
             pltpu.VMEM((local_n, rhs_n * rows, leaf), F32),
             pltpu.VMEM((others, local_n, rows, leaf), BF16),
@@ -273,12 +298,12 @@
             dma((4,)),
             dma((others,)),
             dma((others,)),
+            dma((others, packs)),
+            dma((others, packs)),
             dma((others,)),
             dma((others,)),
-            dma((others,)),
-            dma((others,)),
-            dma((away,)),
-            dma((away,)),
+            dma((clus_n,)),
+            dma((clus_n,)),
             dma((2,)),
             dma((2,)),
         ],

time: 21.6 us -> 20.8 us (0.963)
  Pallas kernels: 20 us -> 19.1 us
    pallas_call x1, Pallas kernels: 20 us -> 19.1 us  [body(): pl.pallas_call(functools.partial(kernel, clus_n, rhs_n), out_shape=jax.Sh...]
where the time goes in v3:
time: 20.8 us; the launch traced here: 20.4 us
  Pallas kernels  19.1 us (92%)
  local copies, waits for them, and re-layouts  1.32 us (6%)
    pallas_call x1, Pallas kernels, body(): pl.pallas_call(functools.partial(kernel, clus_n, rhs_n), out_shape=jax.Sh...  19.1 us
    unnamed x1, local copies, waits for them, and re-layouts  1.32 us

profile of v3, /device:TPU:0, one launch (start us, length us, event | category | flops | bytes accessed | tf_op | source)
XLA Modules:
  0.0 20.4 jit_solution(11563466306881987392)
XLA Ops:
  0.0 19.1 %shard_map.82 = bf16[2,8,512]{2,1,0:T(8,128)(2,1)} custom-call(s32[2]{0:T(128)} %rank_ref.1, s32[2,6]{1,0:T(2,128)} %fcol_ref.1, s32[2,4]{1,0:T(2,128)} %ncol_ref.1, bf16[2,8,512]{2,1,0:T(8,128)(2,1)} %x_ref.1, bf16[2,192,256]{2,1,0:T(8,128)(2,1)} %bitcast.4, bf16[2,6,96,192]{3,2,1,0:T(8,128)(2,1)} %cp_hbm.1, bf16[2,4,512,256]{3,2,1,0:T(8,128)(2,1)} %bitcast.3, ...), custom_call_target="tpu_custom_call" | custom-call | tf_op jit(solution)/shard_map/pallas_call | solution.py:275
  19.1 1.3 %copy.10 = bf16[2,8,512]{2,1,0:T(8,128)(2,1)} copy(bf16[2,8,512]{2,1,0:T(8,128)(2,1)} %shard_map.82) | data formatting | bytes 32768

commit v4 on v3

--- a/solution.py
+++ b/solution.py
@@ -128,7 +128,15 @@
         both = jnp.concatenate(fields[c], axis=1)
         for n in range(near_n):
             prods[c * near_n + n] = jnp.dot(both, nb[c, n], preferred_element_type=F32)
-    for d in range(3):
+    def near_copy(side):
+        other = me_c - 1 if side == 0 else me_c + 1
+        return pltpu.make_async_remote_copy(
+            src_ref=nbs.at[side], dst_ref=nbr.at[1 - side],
+            send_sem=ls_sem.at[side], recv_sem=lr_sem.at[1 - side],
+            device_id={"clus": other}, device_id_type=MESH,
+        )
+
+    def band(d):
         for l in range(local_n):
             place = (d - 1) * local_n + l
             total = None
@@ -144,21 +152,19 @@
             else:
                 nbs[d // 2, l] = total.astype(BF16)
 
-    def near_copy(side):
-        other = me_c - 1 if side == 0 else me_c + 1
-        return pltpu.make_async_remote_copy(
-            src_ref=nbs.at[side], dst_ref=nbr.at[1 - side],
-            send_sem=ls_sem.at[side], recv_sem=lr_sem.at[1 - side],
-            device_id={"clus": other}, device_id_type=MESH,
-        )
+    band(0)
 
     @pl.when(me_c > 0)
     def _():
         near_copy(0).start()
 
+    band(2)
+
     @pl.when(me_c < clus_n - 1)
     def _():
         near_copy(1).start()
+
+    band(1)
 
     def far_copy(g, slot):
         return pltpu.make_async_remote_copy(

time: 20.8 us -> 20.8 us (level)
  no operation moved by 1% of the time
where the time goes in v4:
time: 20.8 us; the launch traced here: 20.4 us
  Pallas kernels  19.1 us (92%)
  local copies, waits for them, and re-layouts  1.32 us (6%)
    pallas_call x1, Pallas kernels, body(): pl.pallas_call(functools.partial(kernel, clus_n, rhs_n), out_shape=jax.Sh...  19.1 us
    unnamed x1, local copies, waits for them, and re-layouts  1.32 us

profile of v4, /device:TPU:0, one launch (start us, length us, event | category | flops | bytes accessed | tf_op | source)
XLA Modules:
  0.0 20.4 jit_solution(3521080983637636561)
XLA Ops:
  0.0 19.1 %shard_map.82 = bf16[2,8,512]{2,1,0:T(8,128)(2,1)} custom-call(s32[2]{0:T(128)} %rank_ref.1, s32[2,6]{1,0:T(2,128)} %fcol_ref.1, s32[2,4]{1,0:T(2,128)} %ncol_ref.1, bf16[2,8,512]{2,1,0:T(8,128)(2,1)} %x_ref.1, bf16[2,192,256]{2,1,0:T(8,128)(2,1)} %bitcast.4, bf16[2,6,96,192]{3,2,1,0:T(8,128)(2,1)} %cp_hbm.1, bf16[2,4,512,256]{3,2,1,0:T(8,128)(2,1)} %bitcast.3, ...), custom_call_target="tpu_custom_call" | custom-call | tf_op jit(solution)/shard_map/pallas_call | solution.py:281
  19.1 1.3 %copy.10 = bf16[2,8,512]{2,1,0:T(8,128)(2,1)} copy(bf16[2,8,512]{2,1,0:T(8,128)(2,1)} %shard_map.82) | data formatting | bytes 32768
